TPU v7x, 128 devices: a whole 4x4x4 slice. The times are simulated.
128 devices in a mesh: tok: 4 (over y), vocab: 32 (over x, z, core).
Axes of the slice: x: 4, y: 4, z: 4, core: 2. Of those that a mesh axis runs over, the one named last changes fastest.
Arguments:
- teacher_logits: bfloat16 [512, 131072], P('tok', 'vocab'), may hold values from -18 to 240
- hidden: bfloat16 [512, 4608], P('tok'), may hold values from -6 to 6
- new_head: bfloat16 [4608, 131072], P(None, ('tok', 'vocab')), may hold values from -0.26516504 to 0.26516504
- labels: int32 [512], replicated, may hold values from 0 to 131071
- map_target: int32 [1024, 4], P('vocab'), may hold values from 0 to 1023, as said below
- map_weight: bfloat16 [1024, 4, 128, 128], P('vocab'), may hold values from 0 to 0.017578125, as said below
Outputs:
- loss: float32 [512], P('tok')
- head_grad: bfloat16 [4608, 131072], P(None, ('tok', 'vocab'))
Inputs may be any that keep to these rules, and one draw needn't show every extreme that they name: `map_target`: values are ids of new blocks; new block b belongs to the device at index b // 8 of tok and vocab together, tok first. Of the 128 entries of one vocab index, at most 2 belong to one device, and some device gets exactly 2. `map_weight`: entries are non-negative.
All inputs are finite; a program needn't handle non-finite values.
Results may differ from a plain program's by a relative error of at most 0.001.
The roundings to bfloat16 on the way count: a program that leaves them out, or rounds other values in their place, can miss the bound.
Values may be sent and summed in bfloat16 or wider, within the bound.
A program may use at most 128 MiB of HBM per device.

v0:
```python
import jax
import jax.numpy as jnp
from jax import lax
from jax.sharding import PartitionSpec as P


def local(teacher_logits, hidden, new_head, labels, map_target, map_weight):
    tok_rows = teacher_logits.shape[0]
    block = map_weight.shape[2]
    fanout = map_weight.shape[1]
    old_blocks = map_target.shape[0]
    entries = old_blocks * fanout
    n_tok = lax.axis_size("tok")
    n_vocab = lax.axis_size("vocab")
    nodes = n_tok * n_vocab
    capacity = max(2, 2 * entries // nodes)
    new_cols = new_head.shape[1]
    per_node = new_cols // block
    own_index = lax.axis_index(("tok", "vocab"))
    scores = teacher_logits.astype(jnp.float32)
    local_top = jnp.max(scores, axis=1)
    highest = lax.pmax(local_top, "vocab")
    total = lax.psum(jnp.sum(jnp.exp(scores - highest[:, None]), axis=1), "vocab")
    teacher_prob = (jnp.exp(scores - highest[:, None]) / total[:, None]).astype(jnp.bfloat16)
    pieces = teacher_prob.reshape(tok_rows, old_blocks, block)
    contrib = jnp.einsum("tjb,jkbc->jktc", pieces, map_weight, preferred_element_type=jnp.float32)
    contrib = contrib.astype(jnp.bfloat16).reshape(entries, tok_rows, block)
    owners = (map_target // per_node).reshape(entries)
    earlier = jnp.arange(entries)[None, :] < jnp.arange(entries)[:, None]
    slots = jnp.sum((owners[:, None] == owners[None, :]) & earlier, axis=1)
    outbox = (
        jnp.zeros((nodes, capacity, tok_rows, block), jnp.bfloat16).at[owners, slots].set(contrib)
    )
    inbox = lax.all_to_all(outbox, ("tok", "vocab"), split_axis=0, concat_axis=0, tiled=True)
    inbox = inbox.reshape(n_tok, n_vocab, capacity, tok_rows, block)
    targets_all = lax.all_gather(map_target, "vocab", axis=0, tiled=True).reshape(n_vocab, entries)
    owners_all = targets_all // per_node
    local_block = targets_all % per_node
    slots_all = jnp.sum((owners_all[:, :, None] == owners_all[:, None, :]) & earlier[None], axis=2)
    picked = (owners_all == own_index)[:, :, None] & (
        slots_all[:, :, None] == jnp.arange(capacity)[None, None, :]
    )
    block_hit = local_block[:, :, None] == jnp.arange(per_node)[None, None, :]
    landing = jnp.einsum(
        "vec,veb->vcb", picked.astype(jnp.float32), block_hit.astype(jnp.float32)
    ).astype(jnp.bfloat16)
    target = jnp.einsum("vcb,svctk->stbk", landing, inbox, preferred_element_type=jnp.float32)
    target = target.reshape(n_tok * tok_rows, new_cols)
    everyone = lax.all_gather(hidden, "tok", axis=0, tiled=True)
    logits = jnp.dot(everyone, new_head, preferred_element_type=jnp.float32)
    columns = own_index * new_cols + jnp.arange(new_cols, dtype=jnp.int32)
    label_hit = labels[:, None] == columns[None, :]
    label_part = jnp.sum(jnp.where(label_hit, logits, 0.0), axis=1)
    mass_part = jnp.sum(target, axis=1)
    inner_part = jnp.sum(target * logits, axis=1)
    row_top = jnp.max(logits, axis=1)
    top_all = lax.pmax(row_top, ("tok", "vocab"))
    exp_part = jnp.sum(jnp.exp(logits - top_all[:, None]), axis=1)
    total_all, target_mass, inner, label_logit = lax.psum(
        (exp_part, mass_part, inner_part, label_part), ("tok", "vocab")
    )
    log_total = top_all + jnp.log(total_all)
    loss_all = target_mass * log_total - inner + log_total - label_logit
    loss = lax.dynamic_slice_in_dim(loss_all, lax.axis_index("tok") * tok_rows, tok_rows)
    probs = jnp.exp(logits - log_total[:, None])
    grad_logits = (
        (target_mass + 1.0)[:, None] * probs - target - label_hit.astype(jnp.float32)
    ).astype(jnp.bfloat16)
    head_grad = lax.dot_general(
        everyone, grad_logits, (((0,), (0,)), ((), ())), preferred_element_type=jnp.float32
    )
    return (loss, head_grad.astype(jnp.bfloat16))


def solution(mesh):
    return jax.shard_map(
        local,
        mesh=mesh,
        in_specs=(
            P("tok", "vocab"),
            P("tok", None),
            P(None, ("tok", "vocab")),
            P(),
            P("vocab", None),
            P("vocab", None, None, None),
        ),
        out_specs=(P("tok"), P(None, ("tok", "vocab"))),
        check_vma=False,
    )
```

profile of v0, /device:TPU:1, one launch (start us, length us, event | category | flops | bytes accessed | tf_op | source)
XLA Modules:
  0.0 477.8 jit_solution(10782458382185194525)
XLA Ops:
  7.2 0.0 copy-start
  7.2 0.0 all-gather.3.cloned.1.call-start
  7.2 0.7 all-gather.3.cloned.1.call-update
  7.9 0.7 add_select_fusion.2
  8.6 0.1 copy.44
  8.7 0.1 eq.79
  8.8 0.1 reshape.176
  8.9 1.5 reduce_max.23
  10.4 64.8 %pmax.14 = f32[128]{0:T(128)S(1)} all-reduce(bf16[128]{0:T(256)(128)(2,1)S(1)} %reduce_max.23), channel_id=1, replica_groups=mesh['tok'=4,'vocab'=32] {'vocab'}, use_global_device_ids=true, to_apply=%region_2.0 | all-reduce | flops 128 | bytes 768 | tf_op jit(solution)/shard_map/pmax | solution.py:22
  75.2 0.0 copy-done
  75.2 0.5 fusion.7
  75.7 67.0 %psum.35 = f32[128]{0:T(128)S(1)} all-reduce(f32[128]{0:T(128)S(1)} %fusion.7), channel_id=1, replica_groups=mesh['tok'=4,'vocab'=32] {'vocab'}, use_global_device_ids=true, to_apply=%region_4.5 | all-reduce | flops 128 | bytes 1024 | tf_op jit(solution)/shard_map/psum | solution.py:23
  142.7 0.0 copy-start.2
  142.7 0.5 fusion.9
  143.2 0.2 copy.62
  143.5 0.2 convert_reduce_fusion.1
  143.6 1.3 copy-done.2
  144.9 3.2 convolution_convert_fusion.1
  148.1 5.5 %broadcast_in_dim.5 = bf16[128,2,128,128]{3,2,1,0:T(8,128)(2,1)} broadcast(bf16[]{:T(256)} %constant.50.clone.1), dimensions={} | broadcast | bytes 8388610 | tf_op jit(solution)/shard_map/broadcast_in_dim | solution.py:32
  153.6 20.7 %scatter_fusion = bf16[128,2,128,128]{3,2,1,0:T(8,128)(2,1)} fusion(bf16[128,2,128,128]{3,2,1,0:T(8,128)(2,1)} %broadcast_in_dim.5, s32[128]{0:T(128)S(1)} %fusion.26, bf16[128,128,128]{2,1,0:T(8,128)(2,1)} %bitcast.43), kind=kCustom, calls=%fused_computation | custom fusion | bytes 12583936 | tf_op jit(solution)/shard_map/scatter | solution.py:32
  174.4 0.0 copy-start.4
  174.4 5.4 %all-to-all-start = ((bf16[128,2,128,128]{3,2,1,0:T(8,128)(2,1)}), bf16[128,2,128,128]{3,2,1,0:T(8,128)(2,1)}, u32[]{:S(2)}, u32[]{:S(2)}) async-start(bf16[128,2,128,128]{3,2,1,0:T(8,128)(2,1)} %scatter_fusion), calls=%async_computation | async-start | bytes 16777216 | tf_op jit(solution)/shard_map/all_to_all | solution.py:34
  179.8 0.0 copy-done.4
  179.8 117.2 %all-gather = s32[32,32,4]{1,2,0:T(4,128)S(1)} all-gather(s32[1,32,4]{1,2,0:T(4,128)S(1)} %bitcast.47), channel_id=1, replica_groups=mesh['tok'=4,'vocab'=32] {'vocab'}, dimensions={0}, use_global_device_ids=true | all-gather | bytes 16896 | tf_op jit(solution)/shard_map/all_gather | solution.py:36
  297.0 0.1 copy.47
  297.1 0.1 copy.48
  297.2 1.3 convert_reduce_fusion
  298.5 0.2 fusion.8
  298.7 0.0 all-gather.3.cloned.1.call-done
  298.7 10.1 %fusion.27 = (f32[512]{0:T(512)S(1)}, f32[512,1024]{1,0:T(8,128)}) fusion(bf16[512,4608]{1,0:T(8,128)(2,1)} %all-gather.3.cloned.1.call-done, bf16[4608,1024]{1,0:T(8,128)(2,1)} %param.8), kind=kOutput, calls=%fused_computation.64 | convolution fusion | flops 4832361984 | bytes 16254976 | tf_op jit(solution)/shard_map/dot_general | solution.py:50
  308.8 65.0 %pmax.15 = f32[512]{0:T(512)S(1)} all-reduce(f32[512]{0:T(512)S(1)} %get-tuple-element.24), channel_id=1, replica_groups=mesh['tok'=4,'vocab'=32] {'tok','vocab'}, use_global_device_ids=true, to_apply=%region_10.11 | all-reduce | flops 512 | bytes 4096 | tf_op jit(solution)/shard_map/pmax | solution.py:57
  373.8 0.0 all-to-all-done
  373.8 0.0 copy-start.1
  373.9 0.0 copy-start.3
  373.9 8.9 %bitcast_reduce_fusion = (f32[4,128]{1,0:T(4,128)S(1)}, f32[4,128,128,8,1]{2,3,4,1,0:T(8,128)S(1)}) fusion(bf16[32,2,8,1,1]{2,1,0,4,3:T(2,128)(2,1)S(1)} %fusion.8, bf16[4,32,2,128,128]{4,3,2,1,0:T(8,128)(2,1)} %bitcast.5), kind=kOutput, calls=%fused_computation.14 | convolution fusion | flops 67632640 | bytes 10488832 | tf_op jit(solution)/shard_map/vcb,svctk->stbk/dot_general | solution.py:47
  382.8 0.0 copy-done.1
  382.8 0.0 copy-done.3
  382.8 1.2 fusion.6
  384.0 62.9 %all-reduce = (f32[512]{0:T(512)S(1)}, f32[512]{0:T(512)S(1)}, f32[512]{0:T(512)S(1)}, f32[512]{0:T(512)S(1)}) all-reduce(f32[512]{0:T(512)S(1)} %get-tuple-element.13, f32[512]{0:T(512)S(1)} %get-tuple-element.14, f32[512]{0:T(512)S(1)} %get-tuple-element.12, f32[512]{0:T(512)S(1)} %bitcast.46), channel_id=1, replica_groups=mesh['tok'=4,'vocab'=32] {'tok','vocab'}, use_global_device_ids=true, to_apply=%region_16.17 | all-reduce | flops 2048 | bytes 16384 | tf_op jit(solution)/shard_map/psum | solution.py:59
  446.8 10.9 %fusion.2 = bf16[4608,1024]{0,1:T(8,128)(2,1)} fusion(bf16[512,4608]{1,0:T(8,128)(2,1)} %all-gather.3.cloned.1.call-done, f32[512,1024]{1,0:T(8,128)} %get-tuple-element.25, f32[64,8,8,128]{3,2,1,0:T(8,128)S(1)} %bitcast.42, f32[512]{0:T(512)S(1)} %get-tuple-element.20, f32[512]{0:T(512)S(1)} %get-tuple-element.23, s32[1024]{0:T(1024)S(1)} %iota_add_fusion, ...), kind=kOutput, calls=%fused_computation.4 | convolution fusion | flops 4840226816 | bytes 18360320 | tf_op jit(solution)/shard_map/dot_general | solution.py:69
  457.8 12.6 %copy.54 = bf16[4608,1024]{1,0:T(8,128)(2,1)} copy(bf16[4608,1024]{0,1:T(8,128)(2,1)} %fusion.2) | data formatting | bytes 18874368
  470.4 0.6 dynamic_slice.3
  (6 shorter events, 0.1 us)
Async XLA Ops:
  7.2 68.0 %copy-start = (bf16[128,4096]{1,0:T(8,128)(2,1)S(1)}, bf16[128,4096]{1,0:T(8,128)(2,1)}, u32[]{:S(2)}) copy-start(bf16[128,4096]{1,0:T(8,128)(2,1)} %param.6) | copy-start | bytes 3145732
  7.2 291.5 %all-gather.3.cloned.1.call-start = ((), (), s32[]{:S(2)}) async-start(), calls=%async_computation.1 | async-start | bytes 5898240 | tf_op jit(solution)/shard_map/all_gather | solution.py:49
  142.7 2.2 copy-start.2
  174.4 5.4 %copy-start.4 = (s32[32,4]{0,1:T(4,128)S(1)}, s32[32,4]{0,1:T(4,128)}, u32[]{:S(2)}) copy-start(s32[32,4]{0,1:T(4,128)} %param.10) | copy-start | bytes 1540
  174.4 199.5 %all-to-all-start = ((bf16[128,2,128,128]{3,2,1,0:T(8,128)(2,1)}), bf16[128,2,128,128]{3,2,1,0:T(8,128)(2,1)}, u32[]{:S(2)}, u32[]{:S(2)}) async-start(bf16[128,2,128,128]{3,2,1,0:T(8,128)(2,1)} %scatter_fusion), calls=%async_computation | async-start | bytes 16777216 | tf_op jit(solution)/shard_map/all_to_all | solution.py:34
  373.8 8.9 %copy-start.1 = (f32[512,1024]{1,0:T(8,128)S(1)}, f32[512,1024]{1,0:T(8,128)}, u32[]{:S(2)}) copy-start(f32[512,1024]{1,0:T(8,128)} %get-tuple-element.25) | copy-start | bytes 6291460
  373.9 8.9 %copy-start.3 = (s32[512]{0:T(512)S(1)}, s32[512]{0:T(512)}, u32[]{:S(2)}) copy-start(s32[512]{0:T(512)} %param.9) | copy-start | bytes 6148
Sparse Core Ops, SparseCore 0:
  9.7 55.8 all-gather.2
where the time goes:
time: 479 us; the launch traced here: 478 us
  blocking collectives  377 us (79%)
  local copies, waits for them, and re-layouts  41.4 us (9%)
  matrix products  33.3 us (7%)
  between operations  14.2 us (3%)
  other arithmetic  5.87 us (1%)
  starting transfers between devices  5.46 us (1%)
    all_gather x1, blocking collectives, local(): lax.all_gather(map_target, 'vocab', axis=0, tiled=True)  117 us
    psum x1, blocking collectives, local(): lax.psum(jnp.sum(jnp.exp(scores - highest[:, None]), axis=1), 'vocab')  67 us
    pmax x1, blocking collectives, local(): top_all = lax.pmax(row_top, ('tok', 'vocab'))  65 us
    pmax x1, blocking collectives, local(): highest = lax.pmax(local_top, 'vocab')  64.8 us
    psum x1, blocking collectives, local(): lax.psum((exp_part, mass_part, inner_part, label_part), ('tok', 'vocab'))  62.9 us
    scatter x1, local copies, waits for them, and re-layouts, local(): jnp.zeros((nodes, capacity, tok_rows, block), jnp.bfloat16)  20.7 us
    unnamed x12, local copies, waits for them, and re-layouts  14.1 us
    dot_general x1, matrix products, local(): lax.dot_general(everyone, grad_logits, (((0,), (0,)), ((), ())), preferre...  10.9 us
  transfers between devices with their start and end apart: 2, of which 0 were waited for; matrix products, arithmetic and copies ran while one was open for 9% of the time, Pallas kernels for 0%

commit v1 on v0

--- a/solution.py
+++ b/solution.py
@@ -20,7 +20,9 @@
     scores = teacher_logits.astype(jnp.float32)
     local_top = jnp.max(scores, axis=1)
     highest = lax.pmax(local_top, "vocab")
-    total = lax.psum(jnp.sum(jnp.exp(scores - highest[:, None]), axis=1), "vocab")
+    total = jnp.sum(
+        lax.all_gather(jnp.sum(jnp.exp(scores - highest[:, None]), axis=1), "vocab"), axis=0
+    )
     teacher_prob = (jnp.exp(scores - highest[:, None]) / total[:, None]).astype(jnp.bfloat16)
     pieces = teacher_prob.reshape(tok_rows, old_blocks, block)
     contrib = jnp.einsum("tjb,jkbc->jktc", pieces, map_weight, preferred_element_type=jnp.float32)

time: 479 us -> 438 us (0.914)
  blocking collectives: 377 us -> 332 us
    psum x1 -> x0, blocking collectives: 67 us -> none  [local(): lax.psum(jnp.sum(jnp.exp(scores - highest[:, None]), axis=1), 'vocab')]
    all_gather x0 -> x1, blocking collectives: none -> 22.2 us  [local(): lax.all_gather(jnp.sum(jnp.exp(scores - highest[:, None]), axis=1), 'vocab')]
  transfers between devices with their start and end apart: 2 -> 2, of which waited for: 0 -> 0; matrix products, arithmetic and copies ran while one was open for 9% -> 10% of each run, Pallas kernels for 0% -> 0%
where the time goes in v1:
time: 438 us; the launch traced here: 437 us
  blocking collectives  332 us (76%)
  local copies, waits for them, and re-layouts  41.4 us (9%)
  matrix products  33.3 us (8%)
  between operations  14.2 us (3%)
  starting transfers between devices  9.62 us (2%)
  other arithmetic  5.92 us (1%)
    all_gather x1, blocking collectives, local(): lax.all_gather(map_target, 'vocab', axis=0, tiled=True)  117 us
    pmax x1, blocking collectives, local(): highest = lax.pmax(local_top, 'vocab')  64.8 us
    pmax x1, blocking collectives, local(): top_all = lax.pmax(row_top, ('tok', 'vocab'))  64.4 us
    psum x1, blocking collectives, local(): lax.psum((exp_part, mass_part, inner_part, label_part), ('tok', 'vocab'))  63.1 us
    all_gather x1, blocking collectives, local(): lax.all_gather(jnp.sum(jnp.exp(scores - highest[:, None]), axis=1), 'vocab')  22.2 us
    scatter x1, local copies, waits for them, and re-layouts, local(): jnp.zeros((nodes, capacity, tok_rows, block), jnp.bfloat16)  20.7 us
    unnamed x12, local copies, waits for them, and re-layouts  14.1 us
    dot_general x1, matrix products, local(): lax.dot_general(everyone, grad_logits, (((0,), (0,)), ((), ())), preferre...  11 us
  transfers between devices with their start and end apart: 2, of which 0 were waited for; matrix products, arithmetic and copies ran while one was open for 10% of the time, Pallas kernels for 0%

profile of v1, /device:TPU:1, one launch (start us, length us, event | category | flops | bytes accessed | tf_op | source)
XLA Modules:
  0.0 437.0 jit_solution(477236080882885919)
XLA Ops:
  7.2 0.0 copy-start
  7.2 0.0 all-gather.5.cloned.1.call-start
  7.2 0.7 all-gather.5.cloned.1.call-update
  7.9 0.7 add_select_fusion.2
  8.6 0.1 copy.44
  8.7 0.1 eq.79
  8.8 0.1 reshape.176
  8.9 1.5 reduce_max.23
  10.4 64.8 %pmax.14 = f32[128]{0:T(128)S(1)} all-reduce(bf16[128]{0:T(256)(128)(2,1)S(1)} %reduce_max.23), channel_id=1, replica_groups=mesh['tok'=4,'vocab'=32] {'vocab'}, use_global_device_ids=true, to_apply=%region_2.0 | all-reduce | flops 128 | bytes 768 | tf_op jit(solution)/shard_map/pmax | solution.py:22
  75.2 0.0 copy-done
  75.2 0.5 fusion.7
  75.7 22.2 %all-gather.1 = f32[32,1,128]{2,1,0:T(1,128)S(1)} all-gather(f32[1,1,128]{2,1,0:T(1,128)S(1)} %bitcast.49), channel_id=2, replica_groups=mesh['tok'=4,'vocab'=32] {'vocab'}, dimensions={0}, use_global_device_ids=true | all-gather | bytes 16896 | tf_op jit(solution)/shard_map/all_gather | solution.py:24
  97.9 0.1 reduce_sum.79
  97.9 0.0 copy-start.2
  97.9 0.5 fusion.9
  98.4 0.2 copy.62
  98.7 0.2 convert_reduce_fusion.1
  98.8 1.3 copy-done.2
  100.1 3.2 convolution_convert_fusion.1
  103.3 5.5 %broadcast_in_dim.5 = bf16[128,2,128,128]{3,2,1,0:T(8,128)(2,1)} broadcast(bf16[]{:T(256)} %constant.50.clone.1), dimensions={} | broadcast | bytes 8388610 | tf_op jit(solution)/shard_map/broadcast_in_dim | solution.py:34
  108.8 20.7 %scatter_fusion = bf16[128,2,128,128]{3,2,1,0:T(8,128)(2,1)} fusion(bf16[128,2,128,128]{3,2,1,0:T(8,128)(2,1)} %broadcast_in_dim.5, s32[128]{0:T(128)S(1)} %fusion.26, bf16[128,128,128]{2,1,0:T(8,128)(2,1)} %bitcast.44), kind=kCustom, calls=%fused_computation | custom fusion | bytes 12583936 | tf_op jit(solution)/shard_map/scatter | solution.py:34
  129.6 0.0 copy-start.4
  129.6 9.6 %all-to-all-start = ((bf16[128,2,128,128]{3,2,1,0:T(8,128)(2,1)}), bf16[128,2,128,128]{3,2,1,0:T(8,128)(2,1)}, u32[]{:S(2)}, u32[]{:S(2)}) async-start(bf16[128,2,128,128]{3,2,1,0:T(8,128)(2,1)} %scatter_fusion), calls=%async_computation | async-start | bytes 16777216 | tf_op jit(solution)/shard_map/all_to_all | solution.py:36
  139.2 0.0 copy-done.4
  139.2 117.3 %all-gather.2 = s32[32,32,4]{1,2,0:T(4,128)S(1)} all-gather(s32[1,32,4]{1,2,0:T(4,128)S(1)} %bitcast.48), channel_id=1, replica_groups=mesh['tok'=4,'vocab'=32] {'vocab'}, dimensions={0}, use_global_device_ids=true | all-gather | bytes 16896 | tf_op jit(solution)/shard_map/all_gather | solution.py:38
  256.5 0.1 copy.47
  256.6 0.1 copy.48
  256.7 1.3 convert_reduce_fusion
  258.0 0.2 fusion.8
  258.2 0.0 all-gather.5.cloned.1.call-done
  258.2 10.1 %fusion.27 = (f32[512]{0:T(512)S(1)}, f32[512,1024]{1,0:T(8,128)}) fusion(bf16[512,4608]{1,0:T(8,128)(2,1)} %all-gather.5.cloned.1.call-done, bf16[4608,1024]{1,0:T(8,128)(2,1)} %param.8), kind=kOutput, calls=%fused_computation.64 | convolution fusion | flops 4832361984 | bytes 16254976 | tf_op jit(solution)/shard_map/dot_general | solution.py:52
  268.3 64.4 %pmax.15 = f32[512]{0:T(512)S(1)} all-reduce(f32[512]{0:T(512)S(1)} %get-tuple-element.24), channel_id=1, replica_groups=mesh['tok'=4,'vocab'=32] {'tok','vocab'}, use_global_device_ids=true, to_apply=%region_10.11 | all-reduce | flops 512 | bytes 4096 | tf_op jit(solution)/shard_map/pmax | solution.py:59
  332.7 0.0 all-to-all-done
  332.7 0.0 copy-start.1
  332.7 0.0 copy-start.3
  332.7 8.9 %bitcast_reduce_fusion = (f32[4,128]{1,0:T(4,128)S(1)}, f32[4,128,128,8,1]{2,3,4,1,0:T(8,128)S(1)}) fusion(bf16[32,2,8,1,1]{2,1,0,4,3:T(2,128)(2,1)S(1)} %fusion.8, bf16[4,32,2,128,128]{4,3,2,1,0:T(8,128)(2,1)} %bitcast.6), kind=kOutput, calls=%fused_computation.14 | convolution fusion | flops 67632640 | bytes 10488832 | tf_op jit(solution)/shard_map/vcb,svctk->stbk/dot_general | solution.py:49
  341.6 0.0 copy-done.1
  341.6 0.0 copy-done.3
  341.7 1.2 fusion.6
  342.9 63.1 %all-reduce = (f32[512]{0:T(512)S(1)}, f32[512]{0:T(512)S(1)}, f32[512]{0:T(512)S(1)}, f32[512]{0:T(512)S(1)}) all-reduce(f32[512]{0:T(512)S(1)} %get-tuple-element.13, f32[512]{0:T(512)S(1)} %get-tuple-element.14, f32[512]{0:T(512)S(1)} %get-tuple-element.12, f32[512]{0:T(512)S(1)} %bitcast.47), channel_id=1, replica_groups=mesh['tok'=4,'vocab'=32] {'tok','vocab'}, use_global_device_ids=true, to_apply=%region_16.17 | all-reduce | flops 2048 | bytes 16384 | tf_op jit(solution)/shard_map/psum | solution.py:61
  406.0 11.0 %fusion.2 = bf16[4608,1024]{0,1:T(8,128)(2,1)} fusion(bf16[512,4608]{1,0:T(8,128)(2,1)} %all-gather.5.cloned.1.call-done, f32[512,1024]{1,0:T(8,128)} %get-tuple-element.25, f32[64,8,8,128]{3,2,1,0:T(8,128)S(1)} %bitcast.43, f32[512]{0:T(512)S(1)} %get-tuple-element.20, f32[512]{0:T(512)S(1)} %get-tuple-element.23, s32[1024]{0:T(1024)S(1)} %iota_add_fusion, ...), kind=kOutput, calls=%fused_computation.4 | convolution fusion | flops 4840226816 | bytes 18360320 | tf_op jit(solution)/shard_map/dot_general | solution.py:71
  417.0 12.6 %copy.54 = bf16[4608,1024]{1,0:T(8,128)(2,1)} copy(bf16[4608,1024]{0,1:T(8,128)(2,1)} %fusion.2) | data formatting | bytes 18874368
  429.6 0.6 dynamic_slice.3
  (6 shorter events, 0.1 us)
Async XLA Ops:
  7.2 68.0 %copy-start = (bf16[128,4096]{1,0:T(8,128)(2,1)S(1)}, bf16[128,4096]{1,0:T(8,128)(2,1)}, u32[]{:S(2)}) copy-start(bf16[128,4096]{1,0:T(8,128)(2,1)} %param.6) | copy-start | bytes 3145732
  7.2 251.0 %all-gather.5.cloned.1.call-start = ((), (), s32[]{:S(2)}) async-start(), calls=%async_computation.1 | async-start | bytes 5898240 | tf_op jit(solution)/shard_map/all_gather | solution.py:51
  97.9 2.2 copy-start.2
  129.6 9.6 %copy-start.4 = (s32[32,4]{0,1:T(4,128)S(1)}, s32[32,4]{0,1:T(4,128)}, u32[]{:S(2)}) copy-start(s32[32,4]{0,1:T(4,128)} %param.10) | copy-start | bytes 1540
  129.6 203.2 %all-to-all-start = ((bf16[128,2,128,128]{3,2,1,0:T(8,128)(2,1)}), bf16[128,2,128,128]{3,2,1,0:T(8,128)(2,1)}, u32[]{:S(2)}, u32[]{:S(2)}) async-start(bf16[128,2,128,128]{3,2,1,0:T(8,128)(2,1)} %scatter_fusion), calls=%async_computation | async-start | bytes 16777216 | tf_op jit(solution)/shard_map/all_to_all | solution.py:36
  332.7 8.9 %copy-start.1 = (f32[512,1024]{1,0:T(8,128)S(1)}, f32[512,1024]{1,0:T(8,128)}, u32[]{:S(2)}) copy-start(f32[512,1024]{1,0:T(8,128)} %get-tuple-element.25) | copy-start | bytes 6291460
  332.7 8.9 %copy-start.3 = (s32[512]{0:T(512)S(1)}, s32[512]{0:T(512)}, u32[]{:S(2)}) copy-start(s32[512]{0:T(512)} %param.9) | copy-start | bytes 6148
Sparse Core Ops, SparseCore 0:
  9.7 55.8 all-gather.4
